TPU v7x, 512 devices: a whole 4x4x16 slice. The times are simulated.
512 devices in a mesh: lev: 16 (over y, x_lo, core), lat: 32 (over x_hi, z).
Axes of the slice: x: 4 (x_hi: 2, x_lo: 2; x = x_hi * 2 + x_lo), y: 4, z: 16, core: 2. Of those that a mesh axis runs over, the one named last changes fastest.
Arguments:
- tokens: bfloat16 [32, 192, 192, 512], P('lev', 'lat'), may hold values from -6 to 6
- latent_query: bfloat16 [3, 1024], replicated, may hold values from -48 to 48
- latent_base: bfloat16 [3, 512], replicated, may hold values from -6 to 6
- key_weight: bfloat16 [512, 1024], P('lat'), may hold values from -0.25 to 0.25
- value_weight: bfloat16 [512, 1024], P('lat'), may hold values from -0.25 to 0.25
- out_weight: bfloat16 [1024, 512], P('lat'), may hold values from -0.1875 to 0.1875
- norm_gain: float32 [512], replicated, may hold values from 0.1 to 1.9
- window_qkv: bfloat16 [512, 1536], P('lat'), may hold values from -0.25 to 0.25
- window_proj: bfloat16 [512, 512], P('lat'), may hold values from -0.25 to 0.25
Outputs:
- section_out: bfloat16 [3, 192, 192, 512], P(None, 'lat', 'lev')
All inputs are finite; a program needn't handle non-finite values.
Results may differ from a plain program's by a relative error of at most 0.011.
Values may be sent and summed in bfloat16 or wider, within the bound.
A program may use at most 192 MiB of HBM per device.

v0:
```python
import math

import jax
import jax.numpy as jnp
from jax import lax
from jax.sharding import PartitionSpec as P

HEAD_DIM = 64
LHEADS = 16
LATENTS = 3
WIN_R = 6
WIN_C = 12


def passed_along(block, axis, distance):
    devices = range(lax.axis_size(axis))
    route = [((i - distance) % len(devices), i) for i in devices]
    return lax.ppermute(block, axis, route)


def layer_norm(values, norm_gain):
    floats = values.astype(jnp.float32)
    center = jnp.mean(floats, axis=-1, keepdims=True)
    spread = jnp.mean((floats - center) ** 2, axis=-1, keepdims=True)
    return ((floats - center) * lax.rsqrt(spread + 1e-05) * norm_gain).astype(jnp.bfloat16)


def level_partials(level_rows, latent_query, key_weight, value_weight):
    levels, rows, cols, width = level_rows.shape
    inner = key_weight.shape[1]
    head_dim = inner // LHEADS
    key_rows = jnp.dot(level_rows, key_weight, preferred_element_type=jnp.float32).astype(
        jnp.bfloat16
    )
    value_rows = jnp.dot(level_rows, value_weight, preferred_element_type=jnp.float32).astype(
        jnp.bfloat16
    )
    key_rows = key_rows.reshape(levels, rows, cols, LHEADS, head_dim)
    value_rows = value_rows.reshape(levels, rows, cols, LHEADS, head_dim)
    queries = latent_query.reshape(LATENTS, LHEADS, head_dim)
    scores = jnp.einsum(
        "lhe,trche->ltrch", queries, key_rows, preferred_element_type=jnp.float32
    ) / math.sqrt(head_dim)
    maxima = jnp.max(scores, axis=1)
    weights = jnp.exp(scores - maxima[:, None])
    totals = jnp.sum(weights, axis=1)
    numerator = jnp.einsum("ltrch,trche->lrche", weights, value_rows.astype(jnp.float32))
    return (maxima, totals, numerator.reshape(LATENTS, rows, cols, inner))


def window_attention(windows, allowed, norm_gain, window_qkv, window_proj):
    count, length, width = windows.shape
    heads = width // HEAD_DIM
    normed = layer_norm(windows, norm_gain)
    packed = jnp.dot(normed, window_qkv, preferred_element_type=jnp.float32).astype(jnp.bfloat16)
    queries = packed[..., :width].reshape(count, length, heads, HEAD_DIM)
    keys_all = packed[..., width : 2 * width].reshape(count, length, heads, HEAD_DIM)
    values_all = packed[..., 2 * width :].reshape(count, length, heads, HEAD_DIM)
    scores = jnp.einsum(
        "wihe,wjhe->whij", queries, keys_all, preferred_element_type=jnp.float32
    ) / math.sqrt(HEAD_DIM)
    scores = jnp.where(allowed, scores, -jnp.inf)
    peak = jnp.max(scores, axis=-1, keepdims=True)
    weights = jnp.exp(scores - peak)
    wprobs = (weights / jnp.sum(weights, axis=-1, keepdims=True)).astype(jnp.bfloat16)
    wout = jnp.einsum(
        "whij,wjhe->wihe", wprobs, values_all, preferred_element_type=jnp.float32
    ).astype(jnp.bfloat16)
    wout = wout.reshape(count, length, width)
    result = windows.astype(jnp.float32) + jnp.dot(
        wout, window_proj, preferred_element_type=jnp.float32
    )
    return result.astype(jnp.bfloat16)


def next_rows(latents):
    half = WIN_R // 2
    arrived = passed_along(latents[:, :half], "lat", -1)
    return jnp.concatenate([latents[:, half:], arrived], axis=1)


def next_cols(latents):
    half = WIN_C // 2
    arrived = passed_along(latents[:, :, :half], "lev", -1)
    return jnp.concatenate([latents[:, :, half:], arrived], axis=2)


def on_device(
    tokens,
    latent_query,
    latent_base,
    key_weight,
    value_weight,
    out_weight,
    norm_gain,
    window_qkv,
    window_proj,
):
    key_weight, value_weight, out_weight, window_qkv, window_proj = (
        lax.all_gather(key_weight, "lat", axis=0, tiled=True),
        lax.all_gather(value_weight, "lat", axis=0, tiled=True),
        lax.all_gather(out_weight, "lat", axis=0, tiled=True),
        lax.all_gather(window_qkv, "lat", axis=0, tiled=True),
        lax.all_gather(window_proj, "lat", axis=0, tiled=True),
    )
    level_dev, rows, cols, width = tokens.shape
    inner = key_weight.shape[1]
    head_dim = inner // LHEADS
    block_cols = cols // lax.axis_size("lev")
    level_rows = lax.all_to_all(tokens, "lev", split_axis=2, concat_axis=0, tiled=True)
    maxima, totals, numerator = level_partials(level_rows, latent_query, key_weight, value_weight)
    parted = numerator.reshape(LATENTS, rows, block_cols, LHEADS, head_dim)
    attn = (
        (parted / totals[..., None]).reshape(LATENTS, rows, block_cols, inner).astype(jnp.bfloat16)
    )
    latents = latent_base.astype(jnp.float32)[:, None, None, :] + jnp.dot(
        attn, out_weight, preferred_element_type=jnp.float32
    )
    latents = latents.astype(jnp.bfloat16)
    shifted = next_cols(next_rows(latents))
    win_rows = rows // WIN_R
    length = LATENTS * WIN_R * block_cols
    windows = (
        shifted.reshape(LATENTS, win_rows, WIN_R, block_cols, width)
        .transpose(1, 0, 2, 3, 4)
        .reshape(win_rows, length, width)
    )
    local_rows = jnp.broadcast_to(
        jnp.arange(WIN_R, dtype=jnp.int32)[None, :, None], (LATENTS, WIN_R, block_cols)
    ).reshape(length)
    grid_rows = rows * lax.axis_size("lat")
    first_row = lax.axis_index("lat") * rows
    global_rows = (
        first_row + jnp.arange(win_rows, dtype=jnp.int32)[:, None] * WIN_R + local_rows[None, :]
    )
    region = global_rows >= grid_rows - WIN_R // 2
    allowed = (region[:, :, None] == region[:, None, :])[:, None]
    done = window_attention(windows, allowed, norm_gain, window_qkv, window_proj)
    done = done.reshape(win_rows, LATENTS, WIN_R, block_cols, width).transpose(1, 0, 2, 3, 4)
    return done.reshape(LATENTS, rows, block_cols, width)


def solution(mesh):
    placed = (
        P("lev", "lat", None, None),
        P(),
        P(),
        P("lat", None),
        P("lat", None),
        P("lat", None),
        P(),
        P("lat", None),
        P("lat", None),
    )
    return jax.shard_map(
        on_device,
        mesh=mesh,
        in_specs=placed,
        out_specs=P(None, "lat", "lev", None),
        check_vma=False,
    )
```

profile of v0, /device:TPU:1, one launch (start us, length us, event | category | flops | bytes accessed | tf_op | source)
XLA Modules:
  0.0 588.2 jit_solution(6406249400837890479)
XLA Ops:
  6.5 0.7 all-gather.7.cloned.1.call-update
  7.3 0.7 all-gather.5.cloned.1.call-update
  8.1 0.7 all-gather.9.cloned.1.call-update
  8.7 4.7 copy.30
  13.4 10.5 %all-to-all-start = ((bf16[2,6,192,512]{3,1,0,2:T(8,128)(2,1)}), bf16[2,6,192,512]{3,1,0,2:T(8,128)(2,1)S(1)}, u32[]{:S(2)}, u32[]{:S(2)}) async-start(bf16[2,6,192,512]{3,1,0,2:T(8,128)(2,1)} %copy.30), calls=%async_computation | async-start | bytes 6291456 | tf_op jit(solution)/shard_map/all_to_all | solution.py:110
  24.0 0.5 all-gather.11.cloned.1.call-update
  24.7 73.2 %all_gather.19 = bf16[512,512]{1,0:T(8,128)(2,1)} all-gather(bf16[16,512]{1,0:T(8,128)(2,1)S(1)} %copy-done.2), channel_id=1, replica_groups=mesh['lev'=16,'lat'=32] {'lat'}, dimensions={0}, use_global_device_ids=true | all-gather | bytes 540672 | tf_op jit(solution)/shard_map/all_gather | solution.py:104
  97.9 1.8 copy.31
  99.7 2.7 copy.32
  102.4 2.4 all_to_all.16
  104.7 44.9 %all-gather.7.cloned.1.call-done = bf16[512,1024]{1,0:T(8,128)(2,1)} async-done(((bf16[16,1024]{1,0:T(8,128)(2,1)}), bf16[512,1024]{1,0:T(8,128)(2,1)}) %all-gather.7.cloned.1.call-update) | async-done | bytes 1048592 | tf_op jit(solution)/shard_map/all_gather | solution.py:100
  149.7 6.8 %convolution_convert_fusion = bf16[32,6,12,1024]{3,0,2,1:T(8,128)(2,1)} fusion(bf16[32,6,12,512]{3,0,2,1:T(8,128)(2,1)} %all_to_all.16, bf16[512,1024]{1,0:T(8,128)(2,1)} %all-gather.7.cloned.1.call-done), kind=kOutput, calls=%fused_computation.5 | convolution fusion | flops 2418278400 | bytes 8126464 | tf_op jit(solution)/shard_map/dot_general | solution.py:32
  156.4 13.2 %reshape.226 = bf16[32,6,12,16,64]{4,3,0,2,1:T(8,128)(2,1)} reshape(bf16[32,6,12,1024]{3,0,2,1:T(8,128)(2,1)} %convolution_convert_fusion) | data formatting | bytes 9437184 | tf_op jit(solution)/shard_map/reshape | solution.py:38
  169.6 17.0 %bitcast_reduce_fusion = (f32[3,6,12,16]{0,2,1,3:T(8,128)}, f32[16,32,6,12,3]{1,4,3,2,0:T(4,128)S(1)}) fusion(bf16[3,16,64,1,1]{2,1,0,4,3:T(8,128)(2,1)S(1)} %bitcast.65, bf16[32,6,12,16,64]{4,3,0,2,1:T(8,128)(2,1)} %reshape.226), kind=kOutput, calls=%fused_computation.11 | convolution fusion | flops 14373504 | bytes 5180928 | tf_op jit(solution)/shard_map/lhe,trche->ltrch/dot_general | solution.py:41
  186.6 103.5 %all-gather.5.cloned.1.call-done = bf16[512,1024]{1,0:T(8,128)(2,1)} async-done(((bf16[16,1024]{1,0:T(8,128)(2,1)}), bf16[512,1024]{1,0:T(8,128)(2,1)}) %all-gather.5.cloned.1.call-update) | async-done | bytes 1048592 | tf_op jit(solution)/shard_map/all_gather | solution.py:101
  290.1 7.1 %convolution_convert_fusion.1 = bf16[32,6,12,1024]{3,0,2,1:T(8,128)(2,1)} fusion(bf16[32,6,12,512]{3,0,2,1:T(8,128)(2,1)} %all_to_all.16, bf16[512,1024]{1,0:T(8,128)(2,1)} %all-gather.5.cloned.1.call-done), kind=kOutput, calls=%fused_computation.6 | convolution fusion | flops 2418278400 | bytes 8126464 | tf_op jit(solution)/shard_map/dot_general | solution.py:35
  297.2 3.0 fusion.32
  300.2 0.3 copy.37
  300.5 13.2 %reshape.225 = bf16[32,6,12,16,64]{4,3,0,2,1:T(8,128)(2,1)} reshape(bf16[32,6,12,1024]{3,0,2,1:T(8,128)(2,1)} %convolution_convert_fusion.1) | data formatting | bytes 9437184 | tf_op jit(solution)/shard_map/reshape | solution.py:39
  313.7 6.3 %fusion.8 = bf16[3,6,12,16,64]{4,0,3,2,1:T(4,128)(2,1)S(1)} fusion(f32[3,6,12,16]{0,3,2,1:T(8,128)S(1)} %copy.37, bf16[3,32,6,12,16]{1,0,3,2,4:T(4,128)(2,1)S(1)} %get-tuple-element.6, bf16[32,6,12,16,64]{4,3,0,2,1:T(8,128)(2,1)} %reshape.225), kind=kOutput, calls=%fused_computation.14 | convolution fusion | flops 14598144 | bytes 5395968 | tf_op jit(solution)/shard_map/ltrch,trche->lrche/dot_general | solution.py:47
  320.2 0.6 convert_element_type.78
  320.8 109.7 %all-gather.9.cloned.1.call-done = bf16[1024,512]{1,0:T(8,128)(2,1)} async-done(((bf16[32,512]{1,0:T(8,128)(2,1)}), bf16[1024,512]{1,0:T(8,128)(2,1)}) %all-gather.9.cloned.1.call-update) | async-done | bytes 1048592 | tf_op jit(solution)/shard_map/all_gather | solution.py:102
  430.5 1.7 fusion.10
  432.3 3.7 collective-permute-start
  436.1 2.6 collective-permute-done
  438.7 12.4 %collective-permute-start.1 = (bf16[3,6,6,512]{3,2,1,0:T(8,128)(2,1)S(1)}, bf16[3,6,6,512]{3,2,1,0:T(8,128)(2,1)S(1)}, u32[]{:S(2)}, u32[]{:S(2)}) collective-permute-start(bf16[3,6,6,512]{3,2,1,0:T(8,128)(2,1)S(1)} %get-tuple-element.11), channel_id=1, source_target_pairs={{32,0},{64,32},{96,64},{128,96},{160,128},{192,160},{224,192},{256... | collective-permute-start | bytes 331784 | tf_op jit(solution)/shard_map/ppermute | solution.py:18
  451.2 3.2 collective-permute-done.1
  455.1 119.2 %all-gather.11.cloned.1.call-done = bf16[512,1536]{1,0:T(8,128)(2,1)} async-done(((bf16[16,1536]{1,0:T(8,128)(2,1)}), bf16[512,1536]{1,0:T(8,128)(2,1)}) %all-gather.11.cloned.1.call-update) | async-done | bytes 1572880 | tf_op jit(solution)/shard_map/all_gather | solution.py:103
  574.3 2.0 fusion.5
  576.8 2.0 fusion.36
  578.8 1.8 convolution_convert_fusion.3
  580.9 0.8 reshape_transpose_reshape.4
  (38 shorter events, 2.1 us)
Async XLA Ops:
  6.5 143.1 %all-gather.7.cloned.1.call-start = ((), (), s32[]{:S(2)}) async-start(), calls=%async_computation.2 | async-start | bytes 1081344 | tf_op jit(solution)/shard_map/all_gather | solution.py:100
  7.3 282.8 %all-gather.5.cloned.1.call-start = ((), (), s32[]{:S(2)}) async-start(), calls=%async_computation.1 | async-start | bytes 1081344 | tf_op jit(solution)/shard_map/all_gather | solution.py:101
  8.0 422.5 %all-gather.9.cloned.1.call-start = ((), (), s32[]{:S(2)}) async-start(), calls=%async_computation.3 | async-start | bytes 1081344 | tf_op jit(solution)/shard_map/all_gather | solution.py:102
  13.4 11.1 %copy-start.3 = (bf16[3,1024]{1,0:T(4,128)(2,1)S(1)}, bf16[3,1024]{1,0:T(4,128)(2,1)}, u32[]{:S(2)}) copy-start(bf16[3,1024]{1,0:T(4,128)(2,1)} %param.10) | copy-start | bytes 18436
  13.4 11.2 %copy-start.4 = (bf16[3,512]{1,0:T(4,128)(2,1)S(1)}, bf16[3,512]{1,0:T(4,128)(2,1)}, u32[]{:S(2)}) copy-start(bf16[3,512]{1,0:T(4,128)(2,1)} %param.11) | copy-start | bytes 9220
  13.4 11.2 %copy-start.2 = (bf16[16,512]{1,0:T(8,128)(2,1)S(1)}, bf16[16,512]{1,0:T(8,128)(2,1)}, u32[]{:S(2)}) copy-start(bf16[16,512]{1,0:T(8,128)(2,1)} %param.17) | copy-start | bytes 49156
  13.4 84.5 %all-to-all-start = ((bf16[2,6,192,512]{3,1,0,2:T(8,128)(2,1)}), bf16[2,6,192,512]{3,1,0,2:T(8,128)(2,1)S(1)}, u32[]{:S(2)}, u32[]{:S(2)}) async-start(bf16[2,6,192,512]{3,1,0,2:T(8,128)(2,1)} %copy.30), calls=%async_computation | async-start | bytes 6291456 | tf_op jit(solution)/shard_map/all_to_all | solution.py:110
  24.0 550.4 %all-gather.11.cloned.1.call-start = ((), (), s32[]{:S(2)}) async-start(), calls=%async_computation.4 | async-start | bytes 1622016 | tf_op jit(solution)/shard_map/all_gather | solution.py:103
  290.1 7.1 %copy-start.1 = (f32[3,6,12,16]{0,2,1,3:T(8,128)S(1)}, f32[3,6,12,16]{0,2,1,3:T(8,128)}, u32[]{:S(2)}) copy-start(f32[3,6,12,16]{0,2,1,3:T(8,128)} %get-tuple-element.14) | copy-start | bytes 41476
  432.2 142.1 %copy-start.5 = (f32[512]{0:T(512)S(1)}, f32[512]{0:T(512)}, u32[]{:S(2)}) copy-start(f32[512]{0:T(512)} %param.15) | copy-start | bytes 6148
  432.3 6.4 %collective-permute-start = (bf16[3,3,12,512]{3,2,1,0:T(8,128)(2,1)S(1)}, bf16[3,3,12,512]{3,2,1,0:T(8,128)(2,1)S(1)}, u32[]{:S(2)}, u32[]{:S(2)}) collective-permute-start(bf16[3,3,12,512]{3,2,1,0:T(8,128)(2,1)S(1)} %get-tuple-element.13), channel_id=1, source_target_pairs={{1,0},{2,1},{3,2},{4,3},{5,4},{6,5},{7,6},{8,7},{9,8},{10,9},{11,1... | collective-permute-start | bytes 331784 | tf_op jit(solution)/shard_map/ppermute | solution.py:18
  438.7 15.7 %collective-permute-start.1 = (bf16[3,6,6,512]{3,2,1,0:T(8,128)(2,1)S(1)}, bf16[3,6,6,512]{3,2,1,0:T(8,128)(2,1)S(1)}, u32[]{:S(2)}, u32[]{:S(2)}) collective-permute-start(bf16[3,6,6,512]{3,2,1,0:T(8,128)(2,1)S(1)} %get-tuple-element.11), channel_id=1, source_target_pairs={{32,0},{64,32},{96,64},{128,96},{160,128},{192,160},{224,192},{256... | collective-permute-start | bytes 331784 | tf_op jit(solution)/shard_map/ppermute | solution.py:18
  578.8 1.9 copy-start
Sparse Core Ops, SparseCore 0:
  10.5 139.1 all-gather.6
  152.8 137.2 all-gather.4
  293.2 137.2 all-gather.8
  433.5 140.8 all-gather.10
where the time goes:
time: 598 us; the launch traced here: 588 us
  waiting for transfers between devices  386 us (65%)
  blocking collectives  73.2 us (12%)
  matrix products  44.9 us (8%)
  local copies, waits for them, and re-layouts  40.7 us (7%)
  starting transfers between devices  26.7 us (4%)
  between operations  13.4 us (2%)
    all_gather x1, waiting for transfers between devices, on_device(): lax.all_gather(window_qkv, 'lat', axis=0, tiled=True)  119 us
    all_gather x1, waiting for transfers between devices, on_device(): lax.all_gather(out_weight, 'lat', axis=0, tiled=True)  110 us
    all_gather x1, waiting for transfers between devices, on_device(): lax.all_gather(value_weight, 'lat', axis=0, tiled=True)  103 us
    all_gather x1, blocking collectives, on_device(): lax.all_gather(window_proj, 'lat', axis=0, tiled=True)  73.2 us
    all_gather x1, waiting for transfers between devices, on_device(): lax.all_gather(key_weight, 'lat', axis=0, tiled=True)  44.9 us
    dot_general x1, matrix products, level_partials(): jnp.einsum('lhe,trche->ltrch', queries, key_rows, preferred_element_type=...  17 us
    ppermute x2, starting transfers between devices, passed_along(): return lax.ppermute(block, axis, route)  16.1 us
    reshape x1, local copies, waits for them, and re-layouts, level_partials(): value_rows = value_rows.reshape(levels, rows, cols, LHEADS, head_dim)  13.2 us
  transfers between devices with their start and end apart: 7, of which 6 were waited for; matrix products, arithmetic and copies ran while one was open for 14% of the time, Pallas kernels for 0%

commit v1 on v0

v1 whole, which is shorter than its diff:
```python
import functools

import jax
import jax.numpy as jnp
from jax import lax
from jax.experimental import pallas as pl
from jax.experimental.pallas import tpu as pltpu
from jax.sharding import PartitionSpec as P

MESH = pl.DeviceIdType.MESH
F32 = jnp.float32
BF16 = jnp.bfloat16

HEAD_DIM = 64
LHEADS = 16
LATENTS = 3
WIN_R = 6
WIN_C = 12
WIDTH = 512
INNER = 1024
PATCHES = WIN_R * WIN_C
SHARD = 16
C_Q, C_V, C_O, C_W, C_P, C_END = 0, 128, 640, 1152, 1920, 2176


def dot(a, b):
    return jnp.dot(a, b, preferred_element_type=F32)


def dot_t(a, b):
    return lax.dot_general(a, b, (((1,), (1,)), ((), ())), preferred_element_type=F32)


def iota(shape, dim):
    return lax.broadcasted_iota(jnp.int32, shape, dim)


def pack_weights(mine, q_ref, kw_ref, vw_ref, ow_ref, qkvw_ref, pw_ref, gathered):
    own_head = iota((LHEADS, INNER), 0) == iota((LHEADS, INNER), 1) // HEAD_DIM
    spread = [
        jnp.where(own_head, q_ref[l : l + 1, :].astype(F32), 0.0) for l in range(LATENTS)
    ]
    spread.append(jnp.zeros((128 - LATENTS * LHEADS, INNER), F32))
    spread = jnp.concatenate(spread, axis=0).astype(BF16)
    folded = dot_t(kw_ref[...], spread) * (HEAD_DIM**-0.5)
    high = folded.astype(BF16)
    parts = (high, (folded - high.astype(F32)).astype(BF16))
    for c in range(2):
        gathered[mine, c, :, C_Q:C_V] = parts[c]
        gathered[mine, c, :, C_V:C_O] = vw_ref[:, c * 512 : c * 512 + 512]
        gathered[mine, c, :, C_O:C_W] = ow_ref[c * 16 : c * 16 + 16, :]
        gathered[mine, c, :, C_W:C_P] = qkvw_ref[:, c * 768 : c * 768 + 768]
        gathered[mine, c, :, C_P:C_END] = pw_ref[:, c * 256 : c * 256 + 256]


def regroup_tokens(group, devices, token_rows, floats, outgoing):
    cols = devices * WIN_C
    for k in range(4):
        floats[k, 0:cols] = token_rows[4 * group + k].astype(F32)
        floats[k, cols : cols + 8] = token_rows[4 * group + k, 0:16].astype(F32)[0:8]
    for i in range(devices):
        first = i * WIN_C + WIN_C // 2
        cut = [floats[k, first : first + WIN_C] for k in range(4)]
        outgoing[i, 48 * group : 48 * group + 48] = jnp.concatenate(cut, axis=0).astype(BF16)


def project_levels(g, arrived, gathered, scores, values):
    rows = arrived[pl.ds(g * 4, 4)].reshape(4 * 144, WIDTH)
    folded = jnp.concatenate(
        [gathered[:, c, :, C_Q:C_V].reshape(WIDTH, 128) for c in range(2)], axis=1
    )
    both = dot(rows, folded)
    scores[g] = both[:, :128] + both[:, 128:]
    for c in range(2):
        weight = gathered[:, c, :, C_V:C_O].reshape(WIDTH, 512)
        values[g, :, c * 512 : c * 512 + 512] = dot(rows, weight).astype(BF16)


def level_attention(scores, probs, values, attn):
    groups = scores.shape[0]

    def level(g):
        return scores[g].reshape(8, PATCHES, 128)

    peak = functools.reduce(jnp.maximum, [jnp.max(level(g), axis=0) for g in range(groups)])
    total = jnp.zeros((PATCHES, 128), F32)
    for g in range(groups):
        weights = jnp.exp(level(g) - peak[None])
        total = total + jnp.sum(weights, axis=0)
        scores[g] = weights.reshape(8 * PATCHES, 128)
    scale = 1.0 / total
    for g in range(groups):
        p = (level(g) * scale[None]).reshape(8 * PATCHES, 128)
        high = p.astype(BF16)
        probs[g, :, 0:128] = high
        probs[g, :, 128:256] = (p - high.astype(F32)).astype(BF16)
    head_of = lax.rem(iota((256, 256), 0), 128) - iota((256, 256), 1) // HEAD_DIM
    for l in range(LATENTS):
        for ch in range(INNER // 256):
            one_hot = jnp.where(head_of == l * LHEADS + ch * 4, 1.0, 0.0).astype(BF16)
            acc = jnp.zeros((PATCHES, 256), F32)
            for g in range(groups):
                wide = dot(probs[g], one_hot)
                v = values[g, :, ch * 256 : ch * 256 + 256].astype(F32)
                acc = acc + jnp.sum((wide * v).reshape(8, PATCHES, 256), axis=0)
            attn[l * PATCHES : (l + 1) * PATCHES, ch * 256 : ch * 256 + 256] = acc


def make_latents(attn, base_ref, gathered, latents):
    weight = gathered[:, :, :, C_O:C_W].reshape(INNER, WIDTH)
    mixed = dot(attn[...].astype(BF16), weight).reshape(LATENTS, PATCHES, WIDTH)
    for l in range(LATENTS):
        row = mixed[l] + base_ref[l : l + 1, :].astype(F32)
        latents[l] = row.astype(BF16).astype(F32)


def window_attention(last, window, gain_ref, gathered, packed, mixed, done, out_ref):
    length = LATENTS * PATCHES
    x = window[...]
    center = jnp.mean(x, axis=-1, keepdims=True)
    moved = x - center
    spread = jnp.mean(moved * moved, axis=-1, keepdims=True)
    normed = (moved * lax.rsqrt(spread + 1e-05) * gain_ref[...]).astype(BF16)
    for c in range(2):
        weight = gathered[:, c, :, C_W:C_P].reshape(WIDTH, 768)
        packed[:, c * 768 : c * 768 + 768] = dot(normed, weight).astype(BF16)
    half = PATCHES // 2

    def region(dim):
        return lax.rem(iota((length, length), dim), PATCHES) >= half

    apart = jnp.logical_and(region(0) != region(1), last)
    bias = jnp.where(apart, -1e30, 0.0)
    first = iota((length, 128), 1) < HEAD_DIM
    for pair in range(WIDTH // 128):
        at = pair * 128
        q = packed[:, at : at + 128].astype(F32) * (HEAD_DIM**-0.5)
        k = packed[:, WIDTH + at : WIDTH + at + 128]
        v = packed[:, 2 * WIDTH + at : 2 * WIDTH + at + 128]
        outs = []
        for side in (first, jnp.logical_not(first)):
            s = dot_t(jnp.where(side, q, 0.0).astype(BF16), k) + bias
            w = jnp.exp(s - jnp.max(s, axis=-1, keepdims=True))
            w = (w / jnp.sum(w, axis=-1, keepdims=True)).astype(BF16)
            outs.append(dot(w, v))
        mixed[:, at : at + 128] = jnp.where(first, outs[0], outs[1]).astype(BF16)
    for c in range(2):
        weight = gathered[:, c, :, C_P:C_END].reshape(WIDTH, 256)
        done[:, c * 256 : c * 256 + 256] = x[:, c * 256 : c * 256 + 256] + dot(mixed[...], weight)
    for l in range(LATENTS):
        for r in range(WIN_R):
            at = l * PATCHES + r * WIN_C
            out_ref[l, r] = done[at : at + WIN_C, :].astype(BF16)


def kernel(
    n_lev,
    n_lat,
    tok_ref,
    q_ref,
    base_ref,
    kw_ref,
    vw_ref,
    ow_ref,
    gain_ref,
    qkvw_ref,
    pw_ref,
    out_ref,
    gathered,
    arrived,
    outgoing,
    token_rows,
    floats,
    scores,
    probs,
    values,
    attn,
    latents,
    edge_out,
    edge_in,
    window,
    packed,
    mixed,
    done,
    load_sem,
    own_sem,
    tok_send,
    tok_recv,
    ring_send,
    ring_recv,
    core_send,
    core_recv,
    hop_sems,
    edge_sems,
):
    load = pltpu.make_async_copy(tok_ref, token_rows, load_sem)
    load.start()
    lev, lat = lax.axis_index("lev"), lax.axis_index("lat")
    depth = n_lat // 2
    side, z = lax.div(lat, depth), lax.rem(lat, depth)
    core = lax.rem(lev, 2)
    sibling = lev + 1 - 2 * core

    def at_z(step):
        return lax.rem(z + step + depth, depth)

    up, down = side * depth + at_z(1), side * depth + at_z(-1)
    across = (1 - side) * depth + z
    north, south = lax.rem(lat + n_lat - 1, n_lat), lax.rem(lat + 1, n_lat)

    barrier = pltpu.get_barrier_semaphore()
    for peer in (up, down, across, north, south):
        pl.semaphore_signal(
            barrier, inc=1, device_id={"lev": lev, "lat": peer}, device_id_type=MESH
        )
    for k in range(1, n_lev):
        peer = lax.rem(lev + k, n_lev)
        pl.semaphore_signal(
            barrier, inc=1, device_id={"lev": peer, "lat": lat}, device_id_type=MESH
        )
    pack_weights(lat, q_ref, kw_ref, vw_ref, ow_ref, qkvw_ref, pw_ref, gathered)
    pl.semaphore_wait(barrier, 5 + n_lev - 1)

    def share(shard, half, send, recv, to_lev, to_lat):
        return pltpu.make_async_remote_copy(
            src_ref=gathered.at[shard, half],
            dst_ref=gathered.at[shard, half],
            send_sem=send,
            recv_sem=recv,
            device_id={"lev": to_lev, "lat": to_lat},
            device_id_type=MESH,
        )

    steps = (depth // 2, depth - 1 - depth // 2)

    def shard_at(stream, step):
        return (side if stream == 0 else 1 - side) * depth + at_z(step)

    def ring(way, stream, step, arriving):
        far = step if arriving else step - 1
        shard = shard_at(stream, -far if way == 0 else far)
        where = (way * 2 + stream) * steps[0] + step - 1
        return share(
            shard, core, ring_send.at[where], ring_recv.at[where], lev, up if way == 0 else down
        )

    def to_sibling(shard):
        return share(shard, core, core_send.at[shard], core_recv.at[shard], sibling, lat)

    def from_sibling(shard):
        return share(shard, 1 - core, core_send.at[shard], core_recv.at[shard], sibling, lat)

    crossing = share(lat, core, hop_sems.at[0], hop_sems.at[1], lev, across)
    crossed = share(across, core, hop_sems.at[0], hop_sems.at[1], lev, across)
    crossing.start()
    for way in range(2):
        if steps[way]:
            ring(way, 0, 1, False).start()

    load.wait()
    for group in range(3):
        regroup_tokens(group, n_lev, token_rows, floats, outgoing)
        if group == 0:
            crossed.wait_recv()
            for way in range(2):
                if steps[way]:
                    ring(way, 1, 1, False).start()
            to_sibling(across).start()
    own = pltpu.make_async_copy(outgoing.at[lev], arrived.at[lev], own_sem)
    own.start()

    def tokens(step, arriving):
        peer = lax.rem(lev + (n_lev - step if arriving else step), n_lev)
        return pltpu.make_async_remote_copy(
            src_ref=outgoing.at[peer],
            dst_ref=arrived.at[peer if arriving else lev],
            send_sem=tok_send.at[step],
            recv_sem=tok_recv.at[step],
            device_id={"lev": peer, "lat": lat},
            device_id_type=MESH,
        )

    for step in range(1, n_lev):
        tokens(step, False).start()

    for step in range(1, steps[0] + 1):
        for stream in range(2):
            for way in range(2):
                if step > steps[way]:
                    continue
                ring(way, stream, step, True).wait_recv()
                if step < steps[way]:
                    ring(way, stream, step + 1, False).start()
                to_sibling(shard_at(stream, -step if way == 0 else step)).start()

    own.wait()
    for step in range(1, n_lev):
        tokens(step, True).wait_recv()
    for step in range(depth):
        for stream in range(2):
            if step or stream:
                from_sibling(shard_at(stream, step)).wait_recv()

    def one_group(g, carry):
        project_levels(g, arrived, gathered, scores, values)
        return carry

    lax.fori_loop(0, n_lev // 4, one_group, 0)
    level_attention(scores, probs, values, attn)
    make_latents(attn, base_ref, gathered, latents)

    half = PATCHES // 2
    edge_out[...] = latents[:, 0:48, :].astype(BF16)
    edge = pltpu.make_async_remote_copy(
        src_ref=edge_out,
        dst_ref=edge_in,
        send_sem=edge_sems.at[0],
        recv_sem=edge_sems.at[1],
        device_id={"lev": lev, "lat": north},
        device_id_type=MESH,
    )
    edge.start()
    for l in range(LATENTS):
        window[l * PATCHES : l * PATCHES + half] = latents[l, half:PATCHES]
    edge.wait_recv()
    for l in range(LATENTS):
        window[l * PATCHES + half : (l + 1) * PATCHES] = edge_in[l].astype(F32)[0:half]
    window_attention(
        lat == n_lat - 1, window, gain_ref, gathered, packed, mixed, done, out_ref
    )

    edge.wait_send()
    crossing.wait_send()
    for step in range(1, n_lev):
        tokens(step, False).wait_send()
    for way in range(2):
        for step in range(1, steps[way] + 1):
            for stream in range(2):
                ring(way, stream, step, False).wait_send()
    for step in range(depth):
        for stream in range(2):
            if step or stream:
                to_sibling(shard_at(stream, step)).wait_send()


def on_device(tokens, query, base, key_w, value_w, out_w, gain, qkv_w, proj_w):
    n_lev, n_lat = lax.axis_size("lev"), lax.axis_size("lat")
    levels, rows, cols, width = tokens.shape
    token_rows = tokens.reshape(levels * rows, cols, width)
    length = LATENTS * PATCHES
    groups = n_lev // 4
    vmem = pl.BlockSpec(memory_space=pltpu.VMEM)
    dma = pltpu.SemaphoreType.DMA
    return pl.pallas_call(
        functools.partial(kernel, n_lev, n_lat),
        out_shape=jax.ShapeDtypeStruct((LATENTS, rows, cols // n_lev, width), BF16),
        in_specs=[pl.BlockSpec(memory_space=pl.ANY)] + [vmem] * 8,
        out_specs=vmem,
        scratch_shapes=[
            pltpu.VMEM((n_lat, 2, SHARD, C_END), BF16),
            pltpu.VMEM((n_lev, 144, width), BF16),
            pltpu.VMEM((n_lev, 144, width), BF16),
            pltpu.VMEM(token_rows.shape, BF16),
            pltpu.VMEM((4, cols + 8, width), F32),
            pltpu.VMEM((groups, 576, 128), F32),
            pltpu.VMEM((groups, 576, 256), BF16),
            pltpu.VMEM((groups, 576, INNER), BF16),
            pltpu.VMEM((length, INNER), F32),
            pltpu.VMEM((LATENTS, PATCHES, width), F32),
            pltpu.VMEM((LATENTS, 48, width), BF16),
            pltpu.VMEM((LATENTS, 48, width), BF16),
            pltpu.VMEM((length, width), F32),
            pltpu.VMEM((length, 3 * width), BF16),
            pltpu.VMEM((length, width), BF16),
            pltpu.VMEM((length, width), F32),
            dma,
            dma,
            dma((n_lev,)),
            dma((n_lev,)),
            dma((2 * n_lat,)),
            dma((2 * n_lat,)),
            dma((n_lat,)),
            dma((n_lat,)),
            dma((2,)),
            dma((2,)),
        ],
        compiler_params=pltpu.CompilerParams(
            collective_id=0, has_side_effects=True, vmem_limit_bytes=48 * 1024 * 1024
        ),
        cost_estimate=pl.CostEstimate(
            flops=6_000_000_000, bytes_accessed=8_000_000, transcendentals=1_000_000
        ),
    )(token_rows, query, base, key_w, value_w, out_w, gain.reshape(1, width), qkv_w, proj_w)


def solution(mesh):
    placed = (
        P("lev", "lat", None, None),
        P(),
        P(),
        P("lat", None),
        P("lat", None),
        P("lat", None),
        P(),
        P("lat", None),
        P("lat", None),
    )
    return jax.shard_map(
        on_device,
        mesh=mesh,
        in_specs=placed,
        out_specs=P(None, "lat", "lev", None),
        check_vma=False,
    )
```

time: 598 us -> 76 us (0.13); the launches traced: 588 us -> 75.4 us
  waiting for transfers between devices: 386 us -> 0 us
  blocking collectives: 73.2 us -> 0 us
  Pallas kernels: 0 us -> 67.2 us
  matrix products: 44.9 us -> 0 us
  local copies, waits for them, and re-layouts: 40.7 us -> 8.23 us
  starting transfers between devices: 26.7 us -> 0 us
  between operations: 13.4 us -> 0.02 us
    all_gather x4 -> x0, waiting for transfers between devices: 377 us -> none  [the longest x1 119 us: on_device(): lax.all_gather(window_qkv, 'lat', axis=0, tiled=True)]
    all_gather x1 -> x0, blocking collectives: 73.2 us -> none  [on_device(): lax.all_gather(window_proj, 'lat', axis=0, tiled=True)]
    pallas_call x0 -> x1, Pallas kernels: none -> 67.2 us  [on_device(): pl.pallas_call(functools.partial(kernel, n_lev, n_lat), out_shape=jax.Sha...]
    dot_general x8 -> x0, matrix products: 42.9 us -> none  [the longest x1 17 us: level_partials(): jnp.einsum('lhe,trche->ltrch', queries, key_rows, preferred_element_type=...]
    reshape x3 -> x0, local copies, waits for them, and re-layouts: 26.5 us -> none  [the longest x1 13.2 us: level_partials(): value_rows = value_rows.reshape(levels, rows, cols, LHEADS, head_dim)]
    ppermute x2 -> x0, starting transfers between devices: 16.1 us -> none  [passed_along(): return lax.ppermute(block, axis, route)]
    all_to_all x1 -> x0, starting transfers between devices: 10.5 us -> none  [on_device(): lax.all_to_all(tokens, 'lev', split_axis=2, concat_axis=0, tiled=True)]
    all_to_all x3 -> x0, local copies, waits for them, and re-layouts: 6.83 us -> none  [on_device(): lax.all_to_all(tokens, 'lev', split_axis=2, concat_axis=0, tiled=True)]
  transfers between devices with their start and end apart: 7 -> 0, of which waited for: 6 -> 0; matrix products, arithmetic and copies ran while one was open for 14% -> 0% of each run, Pallas kernels for 0% -> 0%
where the time goes in v1:
time: 76 us; the launch traced here: 75.4 us
  Pallas kernels  67.2 us (88%)
  local copies, waits for them, and re-layouts  8.23 us (11%)
    pallas_call x1, Pallas kernels, on_device(): pl.pallas_call(functools.partial(kernel, n_lev, n_lat), out_shape=jax.Sha...  67.2 us
    unnamed x19, local copies, waits for them, and re-layouts  8.23 us

profile of v1, /device:TPU:1, one launch (start us, length us, event | category | flops | bytes accessed | tf_op | source)
XLA Modules:
  0.0 75.4 jit_solution(8065197565788909125)
XLA Ops:
  0.0 0.0 copy-start
  0.0 1.7 %copy-done = bf16[2,6,192,512]{3,2,1,0:T(8,128)(2,1)S(1)} copy-done((bf16[2,6,192,512]{3,2,1,0:T(8,128)(2,1)S(1)}, bf16[2,6,192,512]{3,2,1,0:T(8,128)(2,1)}, u32[]{:S(2)}) %copy-start) | copy-done | bytes 2359320
  1.7 0.0 copy-start.1
  1.7 0.8 %copy-done.1 = bf16[16,1536]{1,0:T(8,128)(2,1)S(1)} copy-done((bf16[16,1536]{1,0:T(8,128)(2,1)S(1)}, bf16[16,1536]{1,0:T(8,128)(2,1)}, u32[]{:S(2)}) %copy-start.1) | copy-done | bytes 49176
  2.5 0.0 copy-start.2
  2.5 0.8 %copy-done.2 = bf16[16,1024]{1,0:T(8,128)(2,1)S(1)} copy-done((bf16[16,1024]{1,0:T(8,128)(2,1)S(1)}, bf16[16,1024]{1,0:T(8,128)(2,1)}, u32[]{:S(2)}) %copy-start.2) | copy-done | bytes 32792
  3.2 0.0 copy-start.3
  3.2 0.8 %copy-done.3 = bf16[16,1024]{1,0:T(8,128)(2,1)S(1)} copy-done((bf16[16,1024]{1,0:T(8,128)(2,1)S(1)}, bf16[16,1024]{1,0:T(8,128)(2,1)}, u32[]{:S(2)}) %copy-start.3) | copy-done | bytes 32792
  4.0 0.0 copy-start.4
  4.0 0.8 %copy-done.4 = bf16[32,512]{1,0:T(8,128)(2,1)S(1)} copy-done((bf16[32,512]{1,0:T(8,128)(2,1)S(1)}, bf16[32,512]{1,0:T(8,128)(2,1)}, u32[]{:S(2)}) %copy-start.4) | copy-done | bytes 32792
  4.7 0.0 copy-start.5
  4.7 0.7 copy-done.5
  5.5 0.0 copy-start.6
  5.5 0.7 copy-done.6
  6.2 0.0 copy-start.7
  6.2 0.7 copy-done.7
  6.8 0.0 copy-start.8
  6.8 0.7 copy-done.8
  7.5 67.2 %shard_map.91 = bf16[3,6,12,512]{3,2,1,0:T(8,128)(2,1)S(1)} custom-call(bf16[12,192,512]{2,1,0:T(8,128)(2,1)S(1)} %bitcast.2, bf16[3,1024]{1,0:T(4,128)(2,1)S(1)} %copy-done.6, bf16[3,512]{1,0:T(4,128)(2,1)S(1)} %copy-done.7, bf16[16,1024]{1,0:T(8,128)(2,1)S(1)} %copy-done.2, bf16[16,1024]{1,0:T(8,128)(2,1)S(1)} %copy-done.3, bf16[32,512]{1,0:T(8,128)(2,1)S(1)} %copy-done.4, ...), custom_call_target="tpu_custom_call" | custom-call | flops 6000000000 | bytes 8000000 | tf_op jit(solution)/shard_map/pallas_call | solution.py:354
  74.7 0.7 copy.11
Async XLA Ops:
  0.0 1.7 %copy-start = (bf16[2,6,192,512]{3,2,1,0:T(8,128)(2,1)S(1)}, bf16[2,6,192,512]{3,2,1,0:T(8,128)(2,1)}, u32[]{:S(2)}) copy-start(bf16[2,6,192,512]{3,2,1,0:T(8,128)(2,1)} %param.9) | copy-start | bytes 7077892
  1.7 0.8 %copy-start.1 = (bf16[16,1536]{1,0:T(8,128)(2,1)S(1)}, bf16[16,1536]{1,0:T(8,128)(2,1)}, u32[]{:S(2)}) copy-start(bf16[16,1536]{1,0:T(8,128)(2,1)} %qkvw_ref.1) | copy-start | bytes 147460
  2.5 0.8 %copy-start.2 = (bf16[16,1024]{1,0:T(8,128)(2,1)S(1)}, bf16[16,1024]{1,0:T(8,128)(2,1)}, u32[]{:S(2)}) copy-start(bf16[16,1024]{1,0:T(8,128)(2,1)} %kw_ref.1) | copy-start | bytes 98308
  3.2 0.8 %copy-start.3 = (bf16[16,1024]{1,0:T(8,128)(2,1)S(1)}, bf16[16,1024]{1,0:T(8,128)(2,1)}, u32[]{:S(2)}) copy-start(bf16[16,1024]{1,0:T(8,128)(2,1)} %vw_ref.1) | copy-start | bytes 98308
  4.0 0.8 %copy-start.4 = (bf16[32,512]{1,0:T(8,128)(2,1)S(1)}, bf16[32,512]{1,0:T(8,128)(2,1)}, u32[]{:S(2)}) copy-start(bf16[32,512]{1,0:T(8,128)(2,1)} %ow_ref.1) | copy-start | bytes 98308
  4.7 0.7 copy-start.5
  5.5 0.7 copy-start.6
  6.2 0.7 copy-start.7
  6.8 0.7 copy-start.8

commit v2 on v1

v2 whole, which is shorter than its diff:
```python
import functools

import jax
import jax.numpy as jnp
from jax import lax
from jax.experimental import pallas as pl
from jax.experimental.pallas import tpu as pltpu
from jax.sharding import PartitionSpec as P

MESH = pl.DeviceIdType.MESH
F32 = jnp.float32
BF16 = jnp.bfloat16

HEAD_DIM = 64
LHEADS = 16
LATENTS = 3
WIN_R = 6
WIN_C = 12
WIDTH = 512
INNER = 1024
PATCHES = WIN_R * WIN_C
SHARD = 16
THIRDS = 3
PART = PATCHES // THIRDS
GROUPS = PART // 8
C_V, EARLY = 128, 640
C_W, C_P, LATE = 512, 1280, 1536


def dot(a, b):
    return jnp.dot(a, b, preferred_element_type=F32)


def dot_t(a, b):
    return lax.dot_general(a, b, (((1,), (1,)), ((), ())), preferred_element_type=F32)


def iota(shape, dim):
    return lax.broadcasted_iota(jnp.int32, shape, dim)


def columns_of(gathered, half, start, stop):
    parts = [gathered[:, side, half, :, start:stop] for side in range(2)]
    return jnp.concatenate([p.reshape(-1, stop - start) for p in parts], axis=0)


def fold_query(query, key_rows):
    own_head = iota((LHEADS, INNER), 0) == iota((LHEADS, INNER), 1) // HEAD_DIM
    spread = [jnp.where(own_head, query[l : l + 1, :].astype(F32), 0.0) for l in range(LATENTS)]
    spread.append(jnp.zeros((128 - LATENTS * LHEADS, INNER), F32))
    spread = jnp.concatenate(spread, axis=0).astype(BF16)
    folded = dot_t(key_rows[...], spread) * (HEAD_DIM**-0.5)
    high = folded.astype(BF16)
    return high, (folded - high.astype(F32)).astype(BF16)


def regroup_tokens(third, devices, token_rows, floats, outgoing):
    cols = devices * WIN_C
    for k in range(4):
        row = (k // 2) * WIN_R + 2 * third + k % 2
        floats[k, 0:cols] = token_rows[row].astype(F32)
        floats[k, cols : cols + 8] = token_rows[row, 0:16].astype(F32)[0:8]
    for i in range(devices):
        first = i * WIN_C + WIN_C // 2
        cut = [floats[k, first : first + WIN_C] for k in range(4)]
        levels = [
            jnp.concatenate(cut[2 * l : 2 * l + 2], axis=0).reshape(GROUPS, 8, WIDTH)
            for l in range(2)
        ]
        for g in range(GROUPS):
            block = jnp.concatenate([levels[l][g] for l in range(2)], axis=0)
            outgoing[third, i, g] = block.astype(BF16)


def level_attention(third, arrived, early, values, turned, attn):
    devices = arrived.shape[1]
    rows = arrived[third].reshape(devices * 2 * PART, WIDTH)
    folded = jnp.concatenate([columns_of(early, c, 0, C_V) for c in range(2)], axis=1)
    both = dot(rows, folded)
    for c in range(2):
        found = dot(rows, columns_of(early, c, C_V, EARLY)).astype(BF16)
        values[:, :, :, c * 512 : c * 512 + 512] = found.reshape(devices, GROUPS, 16, 512)
    scores = (both[:, :128] + both[:, 128:]).reshape(devices, GROUPS, 2, 8, 128)
    own_patch = iota((8, 256), 0) == lax.rem(iota((8, 256), 1), 8)
    head_of = iota((8, 256), 1) // HEAD_DIM
    for g in range(GROUPS):
        level = scores[:, g].reshape(2 * devices, 8, 128)
        weights = jnp.exp(level - jnp.max(level, axis=0, keepdims=True))
        weights = weights * (1.0 / jnp.sum(weights, axis=0, keepdims=True))
        turned[g] = weights.reshape(256, 128).T
        for quad in range(LHEADS // 4):
            spread = []
            for l in range(LATENTS):
                for h in range(4):
                    at = l * LHEADS + quad * 4 + h
                    row = jnp.broadcast_to(turned[g, at : at + 1, :], (8, 256))
                    spread.append(jnp.where(own_patch, row, 0.0))
            spread = jnp.concatenate(spread, axis=0).astype(BF16)
            v = values[:, g, :, quad * 256 : quad * 256 + 256].reshape(256, 256)
            sums = dot(spread, v).reshape(LATENTS, 4, 8, 256)
            for l in range(LATENTS):
                own = jnp.zeros((8, 256), F32)
                for h in range(4):
                    own = jnp.where(head_of == h, sums[l, h], own)
                attn[third, l, g * 8 : g * 8 + 8, quad * 256 : quad * 256 + 256] = own


def make_latents(thirds, attn, base, late, latents):
    parts = [late[:, side, :, :, 0:C_W].reshape(INNER // 2, WIDTH) for side in range(2)]
    weight = jnp.concatenate(parts, axis=0)
    count = len(thirds) * LATENTS
    rows = attn[thirds[0] : thirds[-1] + 1].reshape(count * PART, INNER).astype(BF16)
    mixed = dot(rows, weight).reshape(count, PART, WIDTH)
    for k, third in enumerate(thirds):
        for l in range(LATENTS):
            row = mixed[k * LATENTS + l] + base[l : l + 1, :].astype(F32)
            latents[l, third * PART : (third + 1) * PART] = row.astype(BF16).astype(F32)


def window_attention(last, window, gain, late, packed, mixed, done, out_ref):
    length = LATENTS * PATCHES
    x = window[...]
    center = jnp.mean(x, axis=-1, keepdims=True)
    moved = x - center
    spread = jnp.mean(moved * moved, axis=-1, keepdims=True)
    normed = (moved * lax.rsqrt(spread + 1e-05) * gain[...]).astype(BF16)
    for c in range(2):
        weight = columns_of(late, c, C_W, C_P)
        packed[:, c * 768 : c * 768 + 768] = dot(normed, weight).astype(BF16)
    half = PATCHES // 2

    def region(dim):
        return lax.rem(iota((length, length), dim), PATCHES) >= half

    apart = jnp.logical_and(region(0) != region(1), last)
    bias = jnp.where(apart, -1e30, 0.0)
    first = iota((length, 128), 1) < HEAD_DIM

    for i in range(WIDTH // 128):
        at = i * 128
        q = packed[:, at : at + 128].astype(F32) * (HEAD_DIM**-0.5)
        k = packed[:, WIDTH + at : WIDTH + at + 128]
        v = packed[:, 2 * WIDTH + at : 2 * WIDTH + at + 128]
        outs = []
        for side in (first, jnp.logical_not(first)):
            s = dot_t(jnp.where(side, q, 0.0).astype(BF16), k) + bias
            w = jnp.exp(s - jnp.max(s, axis=-1, keepdims=True))
            w = (w * (1.0 / jnp.sum(w, axis=-1, keepdims=True))).astype(BF16)
            outs.append(dot(w, v))
        mixed[:, at : at + 128] = jnp.where(first, outs[0], outs[1]).astype(BF16)
    for c in range(2):
        weight = columns_of(late, c, C_P, LATE)
        done[:, c * 256 : c * 256 + 256] = x[:, c * 256 : c * 256 + 256] + dot(mixed[...], weight)
    for l in range(LATENTS):
        for r in range(WIN_R):
            at = l * PATCHES + r * WIN_C
            out_ref[l, r] = done[at : at + WIN_C, :].astype(BF16)


def kernel(
    n_lev,
    n_lat,
    tok_hbm,
    q_hbm,
    base_hbm,
    kw_hbm,
    vw_hbm,
    ow_hbm,
    gain_hbm,
    qkvw_hbm,
    pw_hbm,
    out_ref,
    early,
    late,
    arrived,
    outgoing,
    token_rows,
    floats,
    query,
    base,
    key_rows,
    gain,
    values,
    turned,
    attn,
    latents,
    edge_out,
    edge_in,
    window,
    packed,
    mixed,
    done,
    load_sems,
    tok_send,
    tok_recv,
    ring_send,
    ring_recv,
    core_send,
    core_recv,
    hop_send,
    hop_recv,
    edge_sems,
):
    lev, lat = lax.axis_index("lev"), lax.axis_index("lat")
    depth = n_lat // 2
    side, z = lax.div(lat, depth), lax.rem(lat, depth)
    moves = [(q_hbm, query), (kw_hbm, key_rows), (base_hbm, base), (gain_hbm, gain)]
    for c in range(2):
        moves += [
            (vw_hbm.at[:, c * 512 : c * 512 + 512], early.at[z, side, c, :, C_V:EARLY]),
            (ow_hbm.at[c * 16 : c * 16 + 16], late.at[z, side, c, :, 0:C_W]),
            (qkvw_hbm.at[:, c * 768 : c * 768 + 768], late.at[z, side, c, :, C_W:C_P]),
            (pw_hbm.at[:, c * 256 : c * 256 + 256], late.at[z, side, c, :, C_P:LATE]),
        ]
    few = len(moves)
    for third in range(THIRDS):
        for l in range(2):
            rows = pl.ds(l * WIN_R + 2 * third, 2)
            moves.append((tok_hbm.at[rows], token_rows.at[rows]))
    loads = [pltpu.make_async_copy(*m, load_sems.at[i]) for i, m in enumerate(moves)]
    for load in loads:
        load.start()

    core = lax.rem(lev, 2)
    sibling = lev + 1 - 2 * core

    def at_z(step):
        return lax.rem(z + step + depth, depth)

    up, down = side * depth + at_z(1), side * depth + at_z(-1)
    across = (1 - side) * depth + z
    north, south = lax.rem(lat + n_lat - 1, n_lat), lax.rem(lat + 1, n_lat)

    barrier = pltpu.get_barrier_semaphore()
    for peer in (up, down, across, north, south):
        pl.semaphore_signal(
            barrier, inc=1, device_id={"lev": lev, "lat": peer}, device_id_type=MESH
        )
    for k in range(1, n_lev):
        peer = lax.rem(lev + k, n_lev)
        pl.semaphore_signal(
            barrier, inc=1, device_id={"lev": peer, "lat": lat}, device_id_type=MESH
        )
    for load in loads[:few]:
        load.wait()
    folded = fold_query(query, key_rows)
    for c in range(2):
        early[z, side, c, :, 0:C_V] = folded[c]

    def regroup(third):
        loads[few + 2 * third].wait()
        loads[few + 2 * third + 1].wait()
        regroup_tokens(third, n_lev, token_rows, floats, outgoing)

    regroup(0)
    pl.semaphore_wait(barrier, 5 + n_lev - 1)

    gathers = (early, late)
    steps = depth // 2
    way = 1 - 2 * core
    onward = side * depth + at_z(way)

    chunks = [(which, stream) for stream in range(2) for which in range(2)]

    def piece(chunk, at):
        which, stream = chunk
        return gathers[which].at[at, side if stream == 0 else 1 - side]

    def ring(chunk, step, arriving):
        at = at_z(-way * (step if arriving else step - 1))
        where = chunk[0] * 2 + chunk[1]
        return pltpu.make_async_remote_copy(
            src_ref=piece(chunk, at),
            dst_ref=piece(chunk, at),
            send_sem=ring_send.at[where, step],
            recv_sem=ring_recv.at[where, step],
            device_id={"lev": lev, "lat": onward},
            device_id_type=MESH,
        )

    def exchange(chunk, step, arriving):
        at = at_z(way * step if arriving else -way * step)
        where = chunk[0] * 2 + chunk[1]
        return pltpu.make_async_remote_copy(
            src_ref=piece(chunk, at),
            dst_ref=piece(chunk, at),
            send_sem=core_send.at[where, step],
            recv_sem=core_recv.at[where, step],
            device_id={"lev": sibling, "lat": lat},
            device_id_type=MESH,
        )

    def cross(which, arriving):
        at = 1 - side if arriving else side
        return pltpu.make_async_remote_copy(
            src_ref=gathers[which].at[z, at],
            dst_ref=gathers[which].at[z, at],
            send_sem=hop_send.at[which],
            recv_sem=hop_recv.at[which],
            device_id={"lev": lev, "lat": across},
            device_id_type=MESH,
        )

    def tick(step):
        for chunk in chunks:
            ring(chunk, step, True).wait_recv()
            if step < steps:
                ring(chunk, step + 1, False).start()
                exchange(chunk, step, False).start()

    def tokens(third, step, arriving):
        peer = lax.rem(lev + (n_lev - step if arriving else step), n_lev)
        return pltpu.make_async_remote_copy(
            src_ref=outgoing.at[third, peer],
            dst_ref=arrived.at[third, peer if arriving else lev],
            send_sem=tok_send.at[third, step],
            recv_sem=tok_recv.at[third, step],
            device_id={"lev": peer, "lat": lat},
            device_id_type=MESH,
        )

    def own(third):
        return pltpu.make_async_copy(
            outgoing.at[third, lev], arrived.at[third, lev], tok_send.at[third, 0]
        )

    def send_tokens(third):
        for step in range(1, n_lev):
            tokens(third, step, False).start()
        own(third).start()

    def tokens_here(third):
        own(third).wait()
        for step in range(1, n_lev):
            tokens(third, step, True).wait_recv()

    for which in range(2):
        cross(which, False).start()
    for which in range(2):
        ring((which, 0), 1, False).start()
    send_tokens(0)
    regroup(1)
    send_tokens(1)
    for which in range(2):
        cross(which, True).wait_recv()
        ring((which, 1), 1, False).start()
    tick(1)
    regroup(2)
    send_tokens(2)
    for step in range(2, steps + 1):
        tick(step)
    for step in range(1, steps):
        for chunk in chunks:
            exchange(chunk, step, True).wait_recv()

    for third in range(THIRDS):
        tokens_here(third)
        level_attention(third, arrived, early, values, turned, attn)
        if third == 1:
            make_latents((0, 1), attn, base, late, latents)
            edge_out[...] = latents[:, 0:48, :].astype(BF16)
            edge = pltpu.make_async_remote_copy(
                src_ref=edge_out,
                dst_ref=edge_in,
                send_sem=edge_sems.at[0],
                recv_sem=edge_sems.at[1],
                device_id={"lev": lev, "lat": north},
                device_id_type=MESH,
            )
            edge.start()
    make_latents((2,), attn, base, late, latents)

    half = PATCHES // 2
    for l in range(LATENTS):
        window[l * PATCHES : l * PATCHES + half] = latents[l, half:PATCHES]
    edge.wait_recv()
    for l in range(LATENTS):
        window[l * PATCHES + half : (l + 1) * PATCHES] = edge_in[l].astype(F32)[0:half]
    window_attention(lat == n_lat - 1, window, gain, late, packed, mixed, done, out_ref)

    edge.wait_send()
    for third in range(THIRDS):
        for step in range(1, n_lev):
            tokens(third, step, False).wait_send()
    for which in range(2):
        cross(which, False).wait_send()
    for chunk in chunks:
        for step in range(1, steps + 1):
            ring(chunk, step, False).wait_send()
        for step in range(1, steps):
            exchange(chunk, step, False).wait_send()


def on_device(tokens, query, base, key_w, value_w, out_w, gain, qkv_w, proj_w):
    n_lev, n_lat = lax.axis_size("lev"), lax.axis_size("lat")
    levels, rows, cols, width = tokens.shape
    token_rows = tokens.reshape(levels * rows, cols, width)
    gain_row = gain.reshape(1, width)
    length = LATENTS * PATCHES
    dma = pltpu.SemaphoreType.DMA
    return pl.pallas_call(
        functools.partial(kernel, n_lev, n_lat),
        out_shape=jax.ShapeDtypeStruct((LATENTS, rows, cols // n_lev, width), BF16),
        in_specs=[pl.BlockSpec(memory_space=pltpu.HBM)] * 9,
        out_specs=pl.BlockSpec(memory_space=pltpu.VMEM),
        scratch_shapes=[
            pltpu.VMEM((n_lat // 2, 2, 2, SHARD, EARLY), BF16),
            pltpu.VMEM((n_lat // 2, 2, 2, SHARD, LATE), BF16),
            pltpu.VMEM((THIRDS, n_lev, GROUPS, 16, width), BF16),
            pltpu.VMEM((THIRDS, n_lev, GROUPS, 16, width), BF16),
            pltpu.VMEM(token_rows.shape, BF16),
            pltpu.VMEM((4, cols + 8, width), F32),
            pltpu.VMEM(query.shape, BF16),
            pltpu.VMEM(base.shape, BF16),
            pltpu.VMEM(key_w.shape, BF16),
            pltpu.VMEM(gain_row.shape, F32),
            pltpu.VMEM((n_lev, GROUPS, 16, INNER), BF16),
            pltpu.VMEM((GROUPS, 128, 256), F32),
            pltpu.VMEM((THIRDS, LATENTS, PART, INNER), F32),
            pltpu.VMEM((LATENTS, PATCHES, width), F32),
            pltpu.VMEM((LATENTS, 48, width), BF16),
            pltpu.VMEM((LATENTS, 48, width), BF16),
            pltpu.VMEM((length, width), F32),
            pltpu.VMEM((length, 3 * width), BF16),
            pltpu.VMEM((length, width), BF16),
            pltpu.VMEM((length, width), F32),
            dma((12 + 2 * THIRDS,)),
            dma((THIRDS, n_lev)),
            dma((THIRDS, n_lev)),
            dma((4, n_lat // 4 + 1)),
            dma((4, n_lat // 4 + 1)),
            dma((4, n_lat // 4)),
            dma((4, n_lat // 4)),
            dma((2,)),
            dma((2,)),
            dma((2,)),
        ],
        compiler_params=pltpu.CompilerParams(
            collective_id=0, has_side_effects=True, vmem_limit_bytes=62 * 1024 * 1024
        ),
        cost_estimate=pl.CostEstimate(
            flops=6_000_000_000, bytes_accessed=8_000_000, transcendentals=1_000_000
        ),
    )(token_rows, query, base, key_w, value_w, out_w, gain_row, qkv_w, proj_w)


def solution(mesh):
    placed = (
        P("lev", "lat", None, None),
        P(),
        P(),
        P("lat", None),
        P("lat", None),
        P("lat", None),
        P(),
        P("lat", None),
        P("lat", None),
    )
    return jax.shard_map(
        on_device,
        mesh=mesh,
        in_specs=placed,
        out_specs=P(None, "lat", "lev", None),
        check_vma=False,
    )
```

time: 76 us -> 64.8 us (0.85)
  the two profiles are of different devices: /device:TPU:1 before, /device:TPU:32 now
where the time goes in v2:
time: 64.8 us; the launch traced here: 64.6 us
  Pallas kernels  62.9 us (97%)
  local copies, waits for them, and re-layouts  1.69 us (3%)
    pallas_call x1, Pallas kernels, on_device(): pl.pallas_call(functools.partial(kernel, n_lev, n_lat), out_shape=jax.Sha...  62.9 us
    unnamed x1, local copies, waits for them, and re-layouts  1.69 us

profile of v2, /device:TPU:32, one launch (start us, length us, event | category | flops | bytes accessed | tf_op | source)
XLA Modules:
  0.0 64.6 jit_solution(15579672136220341171)
XLA Ops:
  0.0 62.9 %shard_map.91 = bf16[3,6,12,512]{3,2,1,0:T(8,128)(2,1)} custom-call(bf16[12,192,512]{2,1,0:T(8,128)(2,1)} %bitcast.2, bf16[3,1024]{1,0:T(4,128)(2,1)} %q_hbm.1, bf16[3,512]{1,0:T(4,128)(2,1)} %base_hbm.1, bf16[16,1024]{1,0:T(8,128)(2,1)} %kw_hbm.1, bf16[16,1024]{1,0:T(8,128)(2,1)} %vw_hbm.1, bf16[32,512]{1,0:T(8,128)(2,1)} %ow_hbm.1, f32[1,512]{1,0:T(1,128)} %bitcast.3, ...), custom_call_target="tpu_custom_call" | custom-call | flops 6000000000 | bytes 8000000 | tf_op jit(solution)/shard_map/pallas_call | solution.py:401
  62.9 1.7 %copy.11 = bf16[3,6,12,512]{3,2,1,0:T(8,128)(2,1)} copy(bf16[3,6,12,512]{3,2,1,0:T(8,128)(2,1)} %shard_map.91) | data formatting | bytes 442368

commit v3 on v2

--- a/solution.py
+++ b/solution.py
@@ -23,8 +23,8 @@
 THIRDS = 3
 PART = PATCHES // THIRDS
 GROUPS = PART // 8
-C_V, EARLY = 128, 640
-C_W, C_P, LATE = 512, 1280, 1536
+C_V, EARLY = 128, 1152
+C_P, C_O, LATE = 1536, 2048, 3072
 
 
 def dot(a, b):
@@ -39,19 +39,20 @@
     return lax.broadcasted_iota(jnp.int32, shape, dim)
 
 
-def columns_of(gathered, half, start, stop):
-    parts = [gathered[:, side, half, :, start:stop] for side in range(2)]
+def columns_of(gathered, start, stop):
+    parts = [gathered[:, side, :, start:stop] for side in range(2)]
     return jnp.concatenate([p.reshape(-1, stop - start) for p in parts], axis=0)
 
 
 def fold_query(query, key_rows):
     own_head = iota((LHEADS, INNER), 0) == iota((LHEADS, INNER), 1) // HEAD_DIM
     spread = [jnp.where(own_head, query[l : l + 1, :].astype(F32), 0.0) for l in range(LATENTS)]
-    spread.append(jnp.zeros((128 - LATENTS * LHEADS, INNER), F32))
-    spread = jnp.concatenate(spread, axis=0).astype(BF16)
+    spread.append(jnp.zeros((64 - LATENTS * LHEADS, INNER), F32))
+    spread = jnp.concatenate(spread * 2, axis=0).astype(BF16)
     folded = dot_t(key_rows[...], spread) * (HEAD_DIM**-0.5)
-    high = folded.astype(BF16)
-    return high, (folded - high.astype(F32)).astype(BF16)
+    high = folded.astype(BF16).astype(F32)
+    low = folded - high
+    return jnp.where(iota(folded.shape, 1) < 64, high, low).astype(BF16)
 
 
 def regroup_tokens(third, devices, token_rows, floats, outgoing):
@@ -75,12 +76,12 @@
 def level_attention(third, arrived, early, values, turned, attn):
     devices = arrived.shape[1]
     rows = arrived[third].reshape(devices * 2 * PART, WIDTH)
-    folded = jnp.concatenate([columns_of(early, c, 0, C_V) for c in range(2)], axis=1)
-    both = dot(rows, folded)
+    both = dot(rows, columns_of(early, 0, C_V))
     for c in range(2):
-        found = dot(rows, columns_of(early, c, C_V, EARLY)).astype(BF16)
+        found = dot(rows, columns_of(early, C_V + c * 512, C_V + c * 512 + 512)).astype(BF16)
         values[:, :, :, c * 512 : c * 512 + 512] = found.reshape(devices, GROUPS, 16, 512)
-    scores = (both[:, :128] + both[:, 128:]).reshape(devices, GROUPS, 2, 8, 128)
+    both = both + jnp.concatenate([both[:, 64:], both[:, :64]], axis=1)
+    scores = both.reshape(devices, GROUPS, 2, 8, 128)
     own_patch = iota((8, 256), 0) == lax.rem(iota((8, 256), 1), 8)
     head_of = iota((8, 256), 1) // HEAD_DIM
     for g in range(GROUPS):
@@ -106,7 +107,10 @@
 
 
 def make_latents(thirds, attn, base, late, latents):
-    parts = [late[:, side, :, :, 0:C_W].reshape(INNER // 2, WIDTH) for side in range(2)]
+    parts = []
+    for side in range(2):
+        halves = [late[:, side, :, C_O + c * 512 : C_O + c * 512 + 512] for c in range(2)]
+        parts.append(jnp.stack(halves, axis=1).reshape(INNER // 2, WIDTH))
     weight = jnp.concatenate(parts, axis=0)
     count = len(thirds) * LATENTS
     rows = attn[thirds[0] : thirds[-1] + 1].reshape(count * PART, INNER).astype(BF16)
@@ -125,7 +129,7 @@
     spread = jnp.mean(moved * moved, axis=-1, keepdims=True)
     normed = (moved * lax.rsqrt(spread + 1e-05) * gain[...]).astype(BF16)
     for c in range(2):
-        weight = columns_of(late, c, C_W, C_P)
+        weight = columns_of(late, c * 768, c * 768 + 768)
         packed[:, c * 768 : c * 768 + 768] = dot(normed, weight).astype(BF16)
     half = PATCHES // 2
 
@@ -149,7 +153,7 @@
             outs.append(dot(w, v))
         mixed[:, at : at + 128] = jnp.where(first, outs[0], outs[1]).astype(BF16)
     for c in range(2):
-        weight = columns_of(late, c, C_P, LATE)
+        weight = columns_of(late, C_P + c * 256, C_P + c * 256 + 256)
         done[:, c * 256 : c * 256 + 256] = x[:, c * 256 : c * 256 + 256] + dot(mixed[...], weight)
     for l in range(LATENTS):
         for r in range(WIN_R):
@@ -205,13 +209,13 @@
     depth = n_lat // 2
     side, z = lax.div(lat, depth), lax.rem(lat, depth)
     moves = [(q_hbm, query), (kw_hbm, key_rows), (base_hbm, base), (gain_hbm, gain)]
-    for c in range(2):
-        moves += [
-            (vw_hbm.at[:, c * 512 : c * 512 + 512], early.at[z, side, c, :, C_V:EARLY]),
-            (ow_hbm.at[c * 16 : c * 16 + 16], late.at[z, side, c, :, 0:C_W]),
-            (qkvw_hbm.at[:, c * 768 : c * 768 + 768], late.at[z, side, c, :, C_W:C_P]),
-            (pw_hbm.at[:, c * 256 : c * 256 + 256], late.at[z, side, c, :, C_P:LATE]),
-        ]
+    moves += [
+        (vw_hbm, early.at[z, side, :, C_V:EARLY]),
+        (qkvw_hbm, late.at[z, side, :, 0:C_P]),
+        (pw_hbm, late.at[z, side, :, C_P:C_O]),
+        (ow_hbm.at[0:16], late.at[z, side, :, C_O : C_O + 512]),
+        (ow_hbm.at[16:32], late.at[z, side, :, C_O + 512 : LATE]),
+    ]
     few = len(moves)
     for third in range(THIRDS):
         for l in range(2):
@@ -243,16 +247,13 @@
         )
     for load in loads[:few]:
         load.wait()
-    folded = fold_query(query, key_rows)
-    for c in range(2):
-        early[z, side, c, :, 0:C_V] = folded[c]
+    early[z, side, :, 0:C_V] = fold_query(query, key_rows)
 
     def regroup(third):
         loads[few + 2 * third].wait()
         loads[few + 2 * third + 1].wait()
         regroup_tokens(third, n_lev, token_rows, floats, outgoing)
 
-    regroup(0)
     pl.semaphore_wait(barrier, 5 + n_lev - 1)
 
     gathers = (early, late)
@@ -260,35 +261,38 @@
     way = 1 - 2 * core
     onward = side * depth + at_z(way)
 
-    chunks = [(which, stream) for stream in range(2) for which in range(2)]
-
-    def piece(chunk, at):
-        which, stream = chunk
-        return gathers[which].at[at, side if stream == 0 else 1 - side]
-
-    def ring(chunk, step, arriving):
-        at = at_z(-way * (step if arriving else step - 1))
-        where = chunk[0] * 2 + chunk[1]
+    def side_of(stream, step):
+        if step == steps:
+            return side + core * (1 - 2 * side)
+        return side if stream == 0 else 1 - side
+
+    def ring(which, stream, step, arriving):
+        at = at_z(-way * (step if arriving else step - 1)), side_of(stream, step)
         return pltpu.make_async_remote_copy(
-            src_ref=piece(chunk, at),
-            dst_ref=piece(chunk, at),
-            send_sem=ring_send.at[where, step],
-            recv_sem=ring_recv.at[where, step],
+            src_ref=gathers[which].at[at],
+            dst_ref=gathers[which].at[at],
+            send_sem=ring_send.at[which * 2 + stream, step],
+            recv_sem=ring_recv.at[which * 2 + stream, step],
             device_id={"lev": lev, "lat": onward},
             device_id_type=MESH,
         )
 
-    def exchange(chunk, step, arriving):
-        at = at_z(way * step if arriving else -way * step)
-        where = chunk[0] * 2 + chunk[1]
+    def exchange(which, stream, step, arriving):
+        there = side_of(stream, step)
+        if arriving and step == steps:
+            there = 1 - there
+        at = at_z(way * step if arriving else -way * step), there
         return pltpu.make_async_remote_copy(
-            src_ref=piece(chunk, at),
-            dst_ref=piece(chunk, at),
-            send_sem=core_send.at[where, step],
-            recv_sem=core_recv.at[where, step],
+            src_ref=gathers[which].at[at],
+            dst_ref=gathers[which].at[at],
+            send_sem=core_send.at[which * 2 + stream, step],
+            recv_sem=core_recv.at[which * 2 + stream, step],
             device_id={"lev": sibling, "lat": lat},
             device_id_type=MESH,
         )
+
+    def streams(step):
+        return range(1 if step == steps else 2)
 
     def cross(which, arriving):
         at = 1 - side if arriving else side
@@ -301,12 +305,19 @@
             device_id_type=MESH,
         )
 
-    def tick(step):
-        for chunk in chunks:
-            ring(chunk, step, True).wait_recv()
-            if step < steps:
-                ring(chunk, step + 1, False).start()
-                exchange(chunk, step, False).start()
+    def tick(which, step):
+        for stream in streams(step):
+            ring(which, stream, step, True).wait_recv()
+            if step + 1 < steps:
+                ring(which, stream, step + 1, False).start()
+            exchange(which, stream, step, False).start()
+        if step + 1 == steps:
+            ring(which, 0, steps, False).start()
+
+    def all_shared(which):
+        for step in range(1, steps + 1):
+            for stream in streams(step):
+                exchange(which, stream, step, True).wait_recv()
 
     def tokens(third, step, arriving):
         peer = lax.rem(lev + (n_lev - step if arriving else step), n_lev)
@@ -336,27 +347,29 @@
 
     for which in range(2):
         cross(which, False).start()
+        ring(which, 0, 1, False).start()
+    regroup(0)
+    send_tokens(0)
     for which in range(2):
-        ring((which, 0), 1, False).start()
-    send_tokens(0)
+        cross(which, True).wait_recv()
+        ring(which, 1, 1, False).start()
     regroup(1)
     send_tokens(1)
-    for which in range(2):
-        cross(which, True).wait_recv()
-        ring((which, 1), 1, False).start()
-    tick(1)
+    tick(0, 1)
     regroup(2)
     send_tokens(2)
     for step in range(2, steps + 1):
-        tick(step)
-    for step in range(1, steps):
-        for chunk in chunks:
-            exchange(chunk, step, True).wait_recv()
+        tick(0, step)
+        tick(1, step - 1)
+    all_shared(0)
 
     for third in range(THIRDS):
         tokens_here(third)
         level_attention(third, arrived, early, values, turned, attn)
+        if third == 0:
+            tick(1, steps)
         if third == 1:
+            all_shared(1)
             make_latents((0, 1), attn, base, late, latents)
             edge_out[...] = latents[:, 0:48, :].astype(BF16)
             edge = pltpu.make_async_remote_copy(
@@ -384,11 +397,11 @@
             tokens(third, step, False).wait_send()
     for which in range(2):
         cross(which, False).wait_send()
-    for chunk in chunks:
+    for which in range(2):
         for step in range(1, steps + 1):
-            ring(chunk, step, False).wait_send()
-        for step in range(1, steps):
-            exchange(chunk, step, False).wait_send()
+            for stream in streams(step):
+                ring(which, stream, step, False).wait_send()
+                exchange(which, stream, step, False).wait_send()
 
 
 def on_device(tokens, query, base, key_w, value_w, out_w, gain, qkv_w, proj_w):
@@ -404,8 +417,8 @@
         in_specs=[pl.BlockSpec(memory_space=pltpu.HBM)] * 9,
         out_specs=pl.BlockSpec(memory_space=pltpu.VMEM),
         scratch_shapes=[
-            pltpu.VMEM((n_lat // 2, 2, 2, SHARD, EARLY), BF16),
-            pltpu.VMEM((n_lat // 2, 2, 2, SHARD, LATE), BF16),
+            pltpu.VMEM((n_lat // 2, 2, SHARD, EARLY), BF16),
+            pltpu.VMEM((n_lat // 2, 2, SHARD, LATE), BF16),
             pltpu.VMEM((THIRDS, n_lev, GROUPS, 16, width), BF16),
             pltpu.VMEM((THIRDS, n_lev, GROUPS, 16, width), BF16),
             pltpu.VMEM(token_rows.shape, BF16),
@@ -424,13 +437,13 @@
             pltpu.VMEM((length, 3 * width), BF16),
             pltpu.VMEM((length, width), BF16),
             pltpu.VMEM((length, width), F32),
-            dma((12 + 2 * THIRDS,)),
+            dma((9 + 2 * THIRDS,)),
             dma((THIRDS, n_lev)),
             dma((THIRDS, n_lev)),
             dma((4, n_lat // 4 + 1)),
             dma((4, n_lat // 4 + 1)),
-            dma((4, n_lat // 4)),
-            dma((4, n_lat // 4)),
+            dma((4, n_lat // 4 + 1)),
+            dma((4, n_lat // 4 + 1)),
             dma((2,)),
             dma((2,)),
             dma((2,)),

time: 64.8 us -> 66.4 us (1.025)
  the two profiles are of different devices: /device:TPU:32 before, /device:TPU:1 now
where the time goes in v3:
time: 66.4 us; the launch traced here: 66.2 us
  Pallas kernels  64.5 us (97%)
  local copies, waits for them, and re-layouts  1.69 us (3%)
    pallas_call x1, Pallas kernels, on_device(): pl.pallas_call(functools.partial(kernel, n_lev, n_lat), out_shape=jax.Sha...  64.5 us
    unnamed x1, local copies, waits for them, and re-layouts  1.69 us

profile of v3, /device:TPU:1, one launch (start us, length us, event | category | flops | bytes accessed | tf_op | source)
XLA Modules:
  0.0 66.2 jit_solution(16780939965435671788)
XLA Ops:
  0.0 64.5 %shard_map.91 = bf16[3,6,12,512]{3,2,1,0:T(8,128)(2,1)} custom-call(bf16[12,192,512]{2,1,0:T(8,128)(2,1)} %bitcast.2, bf16[3,1024]{1,0:T(4,128)(2,1)} %q_hbm.1, bf16[3,512]{1,0:T(4,128)(2,1)} %base_hbm.1, bf16[16,1024]{1,0:T(8,128)(2,1)} %kw_hbm.1, bf16[16,1024]{1,0:T(8,128)(2,1)} %vw_hbm.1, bf16[32,512]{1,0:T(8,128)(2,1)} %ow_hbm.1, f32[1,512]{1,0:T(1,128)} %bitcast.3, ...), custom_call_target="tpu_custom_call" | custom-call | flops 6000000000 | bytes 8000000 | tf_op jit(solution)/shard_map/pallas_call | solution.py:414
  64.5 1.7 %copy.11 = bf16[3,6,12,512]{3,2,1,0:T(8,128)(2,1)} copy(bf16[3,6,12,512]{3,2,1,0:T(8,128)(2,1)} %shard_map.91) | data formatting | bytes 442368

commit v4 on v3

--- a/solution.py
+++ b/solution.py
@@ -208,7 +208,12 @@
     lev, lat = lax.axis_index("lev"), lax.axis_index("lat")
     depth = n_lat // 2
     side, z = lax.div(lat, depth), lax.rem(lat, depth)
-    moves = [(q_hbm, query), (kw_hbm, key_rows), (base_hbm, base), (gain_hbm, gain)]
+    moves = []
+    for third in range(THIRDS):
+        for l in range(2):
+            rows = pl.ds(l * WIN_R + 2 * third, 2)
+            moves.append((tok_hbm.at[rows], token_rows.at[rows]))
+    moves += [(q_hbm, query), (kw_hbm, key_rows), (base_hbm, base), (gain_hbm, gain)]
     moves += [
         (vw_hbm, early.at[z, side, :, C_V:EARLY]),
         (qkvw_hbm, late.at[z, side, :, 0:C_P]),
@@ -216,13 +221,9 @@
         (ow_hbm.at[0:16], late.at[z, side, :, C_O : C_O + 512]),
         (ow_hbm.at[16:32], late.at[z, side, :, C_O + 512 : LATE]),
     ]
-    few = len(moves)
-    for third in range(THIRDS):
-        for l in range(2):
-            rows = pl.ds(l * WIN_R + 2 * third, 2)
-            moves.append((tok_hbm.at[rows], token_rows.at[rows]))
     loads = [pltpu.make_async_copy(*m, load_sems.at[i]) for i, m in enumerate(moves)]
-    for load in loads:
+    first = loads[:2] + loads[2 * THIRDS :]
+    for load in first + loads[2 : 2 * THIRDS]:
         load.start()
 
     core = lax.rem(lev, 2)
@@ -245,15 +246,16 @@
         pl.semaphore_signal(
             barrier, inc=1, device_id={"lev": peer, "lat": lat}, device_id_type=MESH
         )
-    for load in loads[:few]:
+
+    def regroup(third):
+        loads[2 * third].wait()
+        loads[2 * third + 1].wait()
+        regroup_tokens(third, n_lev, token_rows, floats, outgoing)
+
+    regroup(0)
+    for load in first[2:]:
         load.wait()
     early[z, side, :, 0:C_V] = fold_query(query, key_rows)
-
-    def regroup(third):
-        loads[few + 2 * third].wait()
-        loads[few + 2 * third + 1].wait()
-        regroup_tokens(third, n_lev, token_rows, floats, outgoing)
-
     pl.semaphore_wait(barrier, 5 + n_lev - 1)
 
     gathers = (early, late)
@@ -348,7 +350,6 @@
     for which in range(2):
         cross(which, False).start()
         ring(which, 0, 1, False).start()
-    regroup(0)
     send_tokens(0)
     for which in range(2):
         cross(which, True).wait_recv()
@@ -409,6 +410,10 @@
     levels, rows, cols, width = tokens.shape
     token_rows = tokens.reshape(levels * rows, cols, width)
     gain_row = gain.reshape(1, width)
+    operands = [
+        pltpu.with_memory_space_constraint(operand, pltpu.HBM)
+        for operand in (token_rows, query, base, key_w, value_w, out_w, gain_row, qkv_w, proj_w)
+    ]
     length = LATENTS * PATCHES
     dma = pltpu.SemaphoreType.DMA
     return pl.pallas_call(
@@ -449,12 +454,12 @@
             dma((2,)),
         ],
         compiler_params=pltpu.CompilerParams(
-            collective_id=0, has_side_effects=True, vmem_limit_bytes=62 * 1024 * 1024
+            collective_id=0, has_side_effects=True, vmem_limit_bytes=44 * 1024 * 1024
         ),
         cost_estimate=pl.CostEstimate(
             flops=6_000_000_000, bytes_accessed=8_000_000, transcendentals=1_000_000
         ),
-    )(token_rows, query, base, key_w, value_w, out_w, gain_row, qkv_w, proj_w)
+    )(*operands)
 
 
 def solution(mesh):

time: 66.4 us -> 64.7 us (0.974)
  local copies, waits for them, and re-layouts: 1.69 us -> 0.72 us
  Pallas kernels: 64.5 us -> 63.8 us
    unnamed x1, local copies, waits for them, and re-layouts: 1.69 us -> 0.72 us
    pallas_call x1, Pallas kernels: 64.5 us -> 63.8 us  [on_device(): pl.pallas_call(functools.partial(kernel, n_lev, n_lat), out_shape=jax.Sha...]
where the time goes in v4:
time: 64.7 us; the launch traced here: 64.5 us
  Pallas kernels  63.8 us (99%)
  local copies, waits for them, and re-layouts  0.72 us (1%)
    pallas_call x1, Pallas kernels, on_device(): pl.pallas_call(functools.partial(kernel, n_lev, n_lat), out_shape=jax.Sha...  63.8 us

profile of v4, /device:TPU:1, one launch (start us, length us, event | category | flops | bytes accessed | tf_op | source)
XLA Modules:
  0.0 64.5 jit_solution(12346562347245131440)
XLA Ops:
  0.0 63.8 %shard_map.91 = bf16[3,6,12,512]{3,2,1,0:T(8,128)(2,1)S(1)} custom-call(bf16[12,192,512]{2,1,0:T(8,128)(2,1)} %bitcast.2, bf16[3,1024]{1,0:T(4,128)(2,1)} %q_hbm.1, bf16[3,512]{1,0:T(4,128)(2,1)} %base_hbm.1, bf16[16,1024]{1,0:T(8,128)(2,1)} %kw_hbm.1, bf16[16,1024]{1,0:T(8,128)(2,1)} %vw_hbm.1, bf16[32,512]{1,0:T(8,128)(2,1)} %ow_hbm.1, f32[1,512]{1,0:T(1,128)} %bitcast.3, ...), custom_call_target="tpu_custom_call" | custom-call | flops 6000000000 | bytes 8000000 | tf_op jit(solution)/shard_map/pallas_call | solution.py:419
  63.8 0.7 %copy.11 = bf16[3,6,12,512]{3,2,1,0:T(8,128)(2,1)} copy(bf16[3,6,12,512]{3,2,1,0:T(8,128)(2,1)S(1)} %shard_map.91) | data formatting | bytes 442368

commit v5 on v4

--- a/solution.py
+++ b/solution.py
@@ -307,14 +307,15 @@
             device_id_type=MESH,
         )
 
-    def tick(which, step):
+    def tick(kinds, step):
         for stream in streams(step):
-            ring(which, stream, step, True).wait_recv()
-            if step + 1 < steps:
-                ring(which, stream, step + 1, False).start()
-            exchange(which, stream, step, False).start()
-        if step + 1 == steps:
-            ring(which, 0, steps, False).start()
+            for which in kinds:
+                ring(which, stream, step, True).wait_recv()
+                if step + 1 < steps:
+                    ring(which, stream, step + 1, False).start()
+                elif step < steps and stream == 1:
+                    ring(which, 0, steps, False).start()
+                exchange(which, stream, step, False).start()
 
     def all_shared(which):
         for step in range(1, steps + 1):
@@ -356,19 +357,19 @@
         ring(which, 1, 1, False).start()
     regroup(1)
     send_tokens(1)
-    tick(0, 1)
+    tick((0, 1), 1)
     regroup(2)
     send_tokens(2)
-    for step in range(2, steps + 1):
-        tick(0, step)
-        tick(1, step - 1)
+    for step in range(2, steps):
+        tick((0, 1), step)
+    tick((0,), steps)
     all_shared(0)
 
     for third in range(THIRDS):
         tokens_here(third)
         level_attention(third, arrived, early, values, turned, attn)
         if third == 0:
-            tick(1, steps)
+            tick((1,), steps)
         if third == 1:
             all_shared(1)
             make_latents((0, 1), attn, base, late, latents)

time: 64.7 us -> 64.6 us (level)
  no operation moved by 1% of the time
where the time goes in v5:
time: 64.6 us; the launch traced here: 64.5 us
  Pallas kernels  63.8 us (99%)
  local copies, waits for them, and re-layouts  0.72 us (1%)
    pallas_call x1, Pallas kernels, on_device(): pl.pallas_call(functools.partial(kernel, n_lev, n_lat), out_shape=jax.Sha...  63.8 us

profile of v5, /device:TPU:1, one launch (start us, length us, event | category | flops | bytes accessed | tf_op | source)
XLA Modules:
  0.0 64.5 jit_solution(17575348103056586330)
XLA Ops:
  0.0 63.8 %shard_map.91 = bf16[3,6,12,512]{3,2,1,0:T(8,128)(2,1)S(1)} custom-call(bf16[12,192,512]{2,1,0:T(8,128)(2,1)} %bitcast.2, bf16[3,1024]{1,0:T(4,128)(2,1)} %q_hbm.1, bf16[3,512]{1,0:T(4,128)(2,1)} %base_hbm.1, bf16[16,1024]{1,0:T(8,128)(2,1)} %kw_hbm.1, bf16[16,1024]{1,0:T(8,128)(2,1)} %vw_hbm.1, bf16[32,512]{1,0:T(8,128)(2,1)} %ow_hbm.1, f32[1,512]{1,0:T(1,128)} %bitcast.3, ...), custom_call_target="tpu_custom_call" | custom-call | flops 6000000000 | bytes 8000000 | tf_op jit(solution)/shard_map/pallas_call | solution.py:420
  63.8 0.7 %copy.11 = bf16[3,6,12,512]{3,2,1,0:T(8,128)(2,1)} copy(bf16[3,6,12,512]{3,2,1,0:T(8,128)(2,1)S(1)} %shard_map.91) | data formatting | bytes 442368

commit v6 on v5

--- a/solution.py
+++ b/solution.py
@@ -24,7 +24,7 @@
 PART = PATCHES // THIRDS
 GROUPS = PART // 8
 C_V, EARLY = 128, 1152
-C_P, C_O, LATE = 1536, 2048, 3072
+C_O, LATE = 512, 1536
 
 
 def dot(a, b):
@@ -109,7 +109,7 @@
 def make_latents(thirds, attn, base, late, latents):
     parts = []
     for side in range(2):
-        halves = [late[:, side, :, C_O + c * 512 : C_O + c * 512 + 512] for c in range(2)]
+        halves = [late[:, side, 1, :, C_O + c * 512 : C_O + c * 512 + 512] for c in range(2)]
         parts.append(jnp.stack(halves, axis=1).reshape(INNER // 2, WIDTH))
     weight = jnp.concatenate(parts, axis=0)
     count = len(thirds) * LATENTS
@@ -129,7 +129,7 @@
     spread = jnp.mean(moved * moved, axis=-1, keepdims=True)
     normed = (moved * lax.rsqrt(spread + 1e-05) * gain[...]).astype(BF16)
     for c in range(2):
-        weight = columns_of(late, c * 768, c * 768 + 768)
+        weight = columns_of(late.at[:, :, 0], c * 768, c * 768 + 768)
         packed[:, c * 768 : c * 768 + 768] = dot(normed, weight).astype(BF16)
     half = PATCHES // 2
 
@@ -153,7 +153,7 @@
             outs.append(dot(w, v))
         mixed[:, at : at + 128] = jnp.where(first, outs[0], outs[1]).astype(BF16)
     for c in range(2):
-        weight = columns_of(late, C_P + c * 256, C_P + c * 256 + 256)
+        weight = columns_of(late.at[:, :, 1], c * 256, c * 256 + 256)
         done[:, c * 256 : c * 256 + 256] = x[:, c * 256 : c * 256 + 256] + dot(mixed[...], weight)
     for l in range(LATENTS):
         for r in range(WIN_R):
@@ -216,10 +216,10 @@
     moves += [(q_hbm, query), (kw_hbm, key_rows), (base_hbm, base), (gain_hbm, gain)]
     moves += [
         (vw_hbm, early.at[z, side, :, C_V:EARLY]),
-        (qkvw_hbm, late.at[z, side, :, 0:C_P]),
-        (pw_hbm, late.at[z, side, :, C_P:C_O]),
-        (ow_hbm.at[0:16], late.at[z, side, :, C_O : C_O + 512]),
-        (ow_hbm.at[16:32], late.at[z, side, :, C_O + 512 : LATE]),
+        (qkvw_hbm, late.at[z, side, 0]),
+        (pw_hbm, late.at[z, side, 1, :, 0:C_O]),
+        (ow_hbm.at[0:16], late.at[z, side, 1, :, C_O : C_O + 512]),
+        (ow_hbm.at[16:32], late.at[z, side, 1, :, C_O + 512 : LATE]),
     ]
     loads = [pltpu.make_async_copy(*m, load_sems.at[i]) for i, m in enumerate(moves)]
     first = loads[:2] + loads[2 * THIRDS :]
@@ -258,7 +258,11 @@
     early[z, side, :, 0:C_V] = fold_query(query, key_rows)
     pl.semaphore_wait(barrier, 5 + n_lev - 1)
 
-    gathers = (early, late)
+    kinds = range(3)
+
+    def part(which, at, there):
+        return early.at[at, there] if which == 0 else late.at[at, there, which - 1]
+
     steps = depth // 2
     way = 1 - 2 * core
     onward = side * depth + at_z(way)
@@ -271,8 +275,8 @@
     def ring(which, stream, step, arriving):
         at = at_z(-way * (step if arriving else step - 1)), side_of(stream, step)
         return pltpu.make_async_remote_copy(
-            src_ref=gathers[which].at[at],
-            dst_ref=gathers[which].at[at],
+            src_ref=part(which, *at),
+            dst_ref=part(which, *at),
             send_sem=ring_send.at[which * 2 + stream, step],
             recv_sem=ring_recv.at[which * 2 + stream, step],
             device_id={"lev": lev, "lat": onward},
@@ -285,8 +289,8 @@
             there = 1 - there
         at = at_z(way * step if arriving else -way * step), there
         return pltpu.make_async_remote_copy(
-            src_ref=gathers[which].at[at],
-            dst_ref=gathers[which].at[at],
+            src_ref=part(which, *at),
+            dst_ref=part(which, *at),
             send_sem=core_send.at[which * 2 + stream, step],
             recv_sem=core_recv.at[which * 2 + stream, step],
             device_id={"lev": sibling, "lat": lat},
@@ -299,17 +303,17 @@
     def cross(which, arriving):
         at = 1 - side if arriving else side
         return pltpu.make_async_remote_copy(
-            src_ref=gathers[which].at[z, at],
-            dst_ref=gathers[which].at[z, at],
+            src_ref=part(which, z, at),
+            dst_ref=part(which, z, at),
             send_sem=hop_send.at[which],
             recv_sem=hop_recv.at[which],
             device_id={"lev": lev, "lat": across},
             device_id_type=MESH,
         )
 
-    def tick(kinds, step):
+    def tick(some, step):
         for stream in streams(step):
-            for which in kinds:
+            for which in some:
                 ring(which, stream, step, True).wait_recv()
                 if step + 1 < steps:
                     ring(which, stream, step + 1, False).start()
@@ -348,20 +352,20 @@
         for step in range(1, n_lev):
             tokens(third, step, True).wait_recv()
 
-    for which in range(2):
+    for which in kinds:
         cross(which, False).start()
         ring(which, 0, 1, False).start()
     send_tokens(0)
-    for which in range(2):
+    for which in kinds:
         cross(which, True).wait_recv()
         ring(which, 1, 1, False).start()
     regroup(1)
     send_tokens(1)
-    tick((0, 1), 1)
+    tick(kinds, 1)
     regroup(2)
     send_tokens(2)
     for step in range(2, steps):
-        tick((0, 1), step)
+        tick(kinds, step)
     tick((0,), steps)
     all_shared(0)
 
@@ -369,9 +373,10 @@
         tokens_here(third)
         level_attention(third, arrived, early, values, turned, attn)
         if third == 0:
-            tick((1,), steps)
+            tick((1, 2), steps)
         if third == 1:
             all_shared(1)
+            all_shared(2)
             make_latents((0, 1), attn, base, late, latents)
             edge_out[...] = latents[:, 0:48, :].astype(BF16)
             edge = pltpu.make_async_remote_copy(
@@ -397,9 +402,9 @@
     for third in range(THIRDS):
         for step in range(1, n_lev):
             tokens(third, step, False).wait_send()
-    for which in range(2):
+    for which in kinds:
         cross(which, False).wait_send()
-    for which in range(2):
+    for which in kinds:
         for step in range(1, steps + 1):
             for stream in streams(step):
                 ring(which, stream, step, False).wait_send()
@@ -424,7 +429,7 @@
         out_specs=pl.BlockSpec(memory_space=pltpu.VMEM),
         scratch_shapes=[
             pltpu.VMEM((n_lat // 2, 2, SHARD, EARLY), BF16),
-            pltpu.VMEM((n_lat // 2, 2, SHARD, LATE), BF16),
+            pltpu.VMEM((n_lat // 2, 2, 2, SHARD, LATE), BF16),
             pltpu.VMEM((THIRDS, n_lev, GROUPS, 16, width), BF16),
             pltpu.VMEM((THIRDS, n_lev, GROUPS, 16, width), BF16),
             pltpu.VMEM(token_rows.shape, BF16),
@@ -446,12 +451,12 @@
             dma((9 + 2 * THIRDS,)),
             dma((THIRDS, n_lev)),
             dma((THIRDS, n_lev)),
-            dma((4, n_lat // 4 + 1)),
-            dma((4, n_lat // 4 + 1)),
-            dma((4, n_lat // 4 + 1)),
-            dma((4, n_lat // 4 + 1)),
-            dma((2,)),
-            dma((2,)),
+            dma((6, n_lat // 4 + 1)),
+            dma((6, n_lat // 4 + 1)),
+            dma((6, n_lat // 4 + 1)),
+            dma((6, n_lat // 4 + 1)),
+            dma((3,)),
+            dma((3,)),
             dma((2,)),
         ],
         compiler_params=pltpu.CompilerParams(

time: 64.6 us -> 61.7 us (0.955)
  Pallas kernels: 63.8 us -> 60.8 us
    pallas_call x1, Pallas kernels: 63.8 us -> 60.8 us  [on_device(): pl.pallas_call(functools.partial(kernel, n_lev, n_lat), out_shape=jax.Sha...]
where the time goes in v6:
time: 61.7 us; the launch traced here: 61.6 us
  Pallas kernels  60.8 us (99%)
  local copies, waits for them, and re-layouts  0.72 us (1%)
    pallas_call x1, Pallas kernels, on_device(): pl.pallas_call(functools.partial(kernel, n_lev, n_lat), out_shape=jax.Sha...  60.8 us

profile of v6, /device:TPU:1, one launch (start us, length us, event | category | flops | bytes accessed | tf_op | source)
XLA Modules:
  0.0 61.6 jit_solution(9691266808671485974)
XLA Ops:
  0.0 60.8 %shard_map.91 = bf16[3,6,12,512]{3,2,1,0:T(8,128)(2,1)S(1)} custom-call(bf16[12,192,512]{2,1,0:T(8,128)(2,1)} %bitcast.2, bf16[3,1024]{1,0:T(4,128)(2,1)} %q_hbm.1, bf16[3,512]{1,0:T(4,128)(2,1)} %base_hbm.1, bf16[16,1024]{1,0:T(8,128)(2,1)} %kw_hbm.1, bf16[16,1024]{1,0:T(8,128)(2,1)} %vw_hbm.1, bf16[32,512]{1,0:T(8,128)(2,1)} %ow_hbm.1, f32[1,512]{1,0:T(1,128)} %bitcast.3, ...), custom_call_target="tpu_custom_call" | custom-call | flops 6000000000 | bytes 8000000 | tf_op jit(solution)/shard_map/pallas_call | solution.py:425
  60.8 0.7 %copy.11 = bf16[3,6,12,512]{3,2,1,0:T(8,128)(2,1)} copy(bf16[3,6,12,512]{3,2,1,0:T(8,128)(2,1)S(1)} %shard_map.91) | data formatting | bytes 442368
